TPU v7x, 32 devices: a whole 2x2x4 slice. The times are simulated.
32 devices in a mesh: ctx: 8 (over z, x), head: 4 (over y, core).
Axes of the slice: x: 2, y: 2, z: 4, core: 2. Of those that a mesh axis runs over, the one named last changes fastest.
Arguments:
- queries: bfloat16 [1024, 4096], P('ctx', 'head'), may hold values from -6 to 6
- keys_new: bfloat16 [1024, 1024], P('ctx', 'head'), may hold values from -6 to 6
- values_new: bfloat16 [1024, 1024], P('ctx', 'head'), may hold values from -6 to 6
- cache_keys: bfloat16 [8192, 1024], P('ctx', 'head'), may hold values from -6 to 6
- cache_values: bfloat16 [8192, 1024], P('ctx', 'head'), may hold values from -6 to 6
- block_list: int32 [8, 8, 16], P('head', 'ctx'), may hold values from -1 to 63, as said below
- block_count: int32 [8, 8], P('head', 'ctx'), may hold values from 0 to 16
- out_weight: bfloat16 [4096, 4096], P('head'), may hold values from -0.21875 to 0.21875
Outputs:
- mixed: bfloat16 [1024, 4096], P(('ctx', 'head'))
Inputs may be any that keep to these rules, and one draw needn't show every extreme that they name: `block_list`: row (h, q) holds distinct cache block numbers in increasing order in its first block_count[h, q] entries and -1 after them. For each KV head, the query blocks of one aligned run of 1 query block together list at most 2 blocks of each aligned run of 8 cache blocks and at least one; for every KV head some run lists exactly 2 of every run of cache blocks.
All inputs are finite; a program needn't handle non-finite values.
Results may differ from a plain program's by a relative error of at most 0.015.
Values may be sent and summed in bfloat16 or wider, within the bound.
A program may use at most 192 MiB of HBM per device.

v0:
```python
import jax
import jax.numpy as jnp
from jax import lax
from jax.sharding import PartitionSpec as P

HD = 128
BLOCK = 128
CAP = 2
CB_DEV = 8


def passed_along(shard, axis, by):
    devices = lax.axis_size(axis)
    pairs = [(i, i + by) for i in range(devices) if 0 <= i + by < devices]
    return lax.ppermute(shard, axis, pairs)


def wanted(block_rows, counts, block_ids):
    in_use = jnp.arange(block_rows.shape[2])[None, None, :] < counts[:, :, None]
    matches = (block_rows[:, :, :, None] == block_ids[None, None, None, :]) & in_use[:, :, :, None]
    return jnp.any(matches, axis=2)


def slot_table(union_mask):
    position = jnp.cumsum(union_mask.astype(jnp.int32), axis=-1) - 1
    return union_mask[:, :, None, :] & (
        position[:, :, None, :] == jnp.arange(CAP)[None, None, :, None]
    )


def shards(
    queries, keys_new, values_new, cache_keys, cache_values, block_list, block_count, out_weight
):
    n_ctx = lax.axis_size("ctx")
    my_index = lax.axis_index("ctx")
    kv_local = keys_new.shape[1] // HD
    group_size = queries.shape[1] // keys_new.shape[1]
    row_count = queries.shape[0]
    qb_dev = row_count // BLOCK
    nblocks = n_ctx * CB_DEV
    slot_count = n_ctx * CAP
    per_query = wanted(block_list, block_count, jnp.arange(nblocks, dtype=jnp.int32))
    union_mask = jnp.any(per_query, axis=1).reshape(kv_local, n_ctx, CB_DEV)
    picker = slot_table(union_mask)
    per_owner = per_query.reshape(kv_local, qb_dev, n_ctx, CB_DEV)
    listed = jnp.any(picker[:, None] & per_owner[:, :, :, None, :], axis=-1).reshape(
        kv_local, qb_dev, slot_count
    )
    same_owner = jnp.arange(n_ctx)[:, None] == jnp.arange(n_ctx)[None, :]
    pick_global = (
        (picker[:, :, :, None, :] & same_owner[None, :, None, :, None])
        .reshape(kv_local, slot_count, nblocks)
        .astype(jnp.bfloat16)
    )
    pieces = (
        lax.all_gather(cache_keys, "ctx", axis=0, tiled=True),
        lax.all_gather(cache_values, "ctx", axis=0, tiled=True),
    )
    piece_blocks = pieces[0].shape[0] // BLOCK
    piece_keys = pieces[0].reshape(piece_blocks, BLOCK, kv_local, HD)
    piece_values = pieces[1].reshape(piece_blocks, BLOCK, kv_local, HD)
    keys_part = jnp.einsum(
        "hsb,bthd->hstd", pick_global, piece_keys, preferred_element_type=jnp.float32
    ).astype(jnp.bfloat16)
    values_part = jnp.einsum(
        "hsb,bthd->hstd", pick_global, piece_values, preferred_element_type=jnp.float32
    ).astype(jnp.bfloat16)
    prev_keys, prev_values = passed_along((keys_new, values_new), "ctx", 1)
    stretch_keys = jnp.concatenate([prev_keys, keys_new], axis=0)
    stretch_values = jnp.concatenate([prev_values, values_new], axis=0)
    row_ids = jnp.arange(row_count)[:, None]
    key_ids = jnp.arange(BLOCK + row_count)[None, :] - BLOCK
    stretch_ok = (
        (key_ids <= row_ids)
        & (key_ids >= (row_ids // BLOCK - 1) * BLOCK)
        & ((my_index > 0) | (key_ids >= 0))
    )
    score_scale = HD ** (-0.5)
    head_outputs = []
    for kv_head in range(kv_local):
        cache_keyhead = keys_part[kv_head].reshape(slot_count * BLOCK, HD)
        cache_valuehead = values_part[kv_head].reshape(slot_count * BLOCK, HD)
        stretch_keyhead = stretch_keys[:, kv_head * HD : (kv_head + 1) * HD]
        stretch_valuehead = stretch_values[:, kv_head * HD : (kv_head + 1) * HD]
        block_ok = listed[kv_head]
        for member in range(group_size):
            column = (kv_head * group_size + member) * HD
            query_head = queries[:, column : column + HD]
            cache_scores = (
                jnp.einsum(
                    "rd,kd->rk", query_head, cache_keyhead, preferred_element_type=jnp.float32
                )
                * score_scale
            )
            cache_scores = jnp.where(
                block_ok[:, None, :, None],
                cache_scores.reshape(qb_dev, BLOCK, slot_count, BLOCK),
                -jnp.inf,
            ).reshape(row_count, slot_count * BLOCK)
            stretch_scores = (
                jnp.einsum(
                    "rd,kd->rk", query_head, stretch_keyhead, preferred_element_type=jnp.float32
                )
                * score_scale
            )
            stretch_scores = jnp.where(stretch_ok, stretch_scores, -jnp.inf)
            row_max = jnp.maximum(jnp.max(cache_scores, axis=1), jnp.max(stretch_scores, axis=1))[
                :, None
            ]
            cache_weights = jnp.exp(cache_scores - row_max)
            stretch_weights = jnp.exp(stretch_scores - row_max)
            weight_sum = jnp.sum(cache_weights, axis=1) + jnp.sum(stretch_weights, axis=1)
            mixture = jnp.dot(
                cache_weights.astype(jnp.bfloat16),
                cache_valuehead,
                preferred_element_type=jnp.float32,
            )
            mixture = mixture + jnp.dot(
                stretch_weights.astype(jnp.bfloat16),
                stretch_valuehead,
                preferred_element_type=jnp.float32,
            )
            head_outputs.append((mixture / weight_sum[:, None]).astype(jnp.bfloat16))
    attention = jnp.concatenate(head_outputs, axis=1)
    mixed = lax.psum_scatter(
        jnp.dot(attention, out_weight, preferred_element_type=jnp.float32).astype(jnp.bfloat16),
        "head",
        scatter_dimension=0,
        tiled=True,
    )
    return mixed


def solution(mesh):
    return jax.shard_map(
        shards,
        mesh=mesh,
        in_specs=(
            P("ctx", "head"),
            P("ctx", "head"),
            P("ctx", "head"),
            P("ctx", "head"),
            P("ctx", "head"),
            P("head", "ctx", None),
            P("head", "ctx"),
            P("head", None),
        ),
        out_specs=P(("ctx", "head"), None),
        check_vma=False,
    )
```

profile of v0, /device:TPU:3, one launch (start us, length us, event | category | flops | bytes accessed | tf_op | source)
XLA Modules:
  0.0 215.8 jit_solution(11331780501026474143)
XLA Ops:
  8.1 3.2 %collective-permute-start = (bf16[128,256]{1,0:T(8,128)(2,1)}, bf16[128,256]{1,0:T(8,128)(2,1)S(1)}, u32[]{:S(2)}, u32[]{:S(2)}) collective-permute-start(bf16[128,256]{1,0:T(8,128)(2,1)} %param.9), channel_id=1, source_target_pairs={{0,4},{4,8},{8,12},{12,16},{16,20},{20,24},{24,28},{1,5},{5,9},{9,... | collective-permute-start | bytes 196616 | tf_op jit(solution)/shard_map/ppermute | solution.py:15
  11.2 3.1 %collective-permute-start.1 = (bf16[128,256]{1,0:T(8,128)(2,1)}, bf16[128,256]{1,0:T(8,128)(2,1)S(1)}, u32[]{:S(2)}, u32[]{:S(2)}) collective-permute-start(bf16[128,256]{1,0:T(8,128)(2,1)} %param.10), channel_id=1, source_target_pairs={{0,4},{4,8},{8,12},{12,16},{16,20},{20,24},{24,28},{1,5},{5,9},{9,... | collective-permute-start | bytes 196616 | tf_op jit(solution)/shard_map/ppermute | solution.py:15
  14.4 0.7 iota_compare_fusion.4
  15.1 0.8 fusion.165
  17.4 0.8 constant_dynamic-update-slice_fusion
  18.3 0.9 constant_dynamic-update-slice_fusion.2
  19.1 2.1 fusion.181
  21.3 2.2 %fusion.183 = (f32[128]{0:T(128)}, f32[128,256]{0,1:T(8,128)}) fusion(bf16[128,1024]{1,0:T(8,128)(2,1)} %param.8, bf16[256,256]{1,0:T(8,128)(2,1)S(1)} %constant_dynamic-update-slice_fusion, pred[256]{0:T(512)(128)(4,1)S(1)} %compare_or_fusion, s32[128]{0:T(128)S(1)} %fusion.176, s32[256]{0:T(256)S(1)} %iota_add_fusion), kind=kOutput, calls=%fused_computation.223 | convolution fusion | flops 8617856 | bytes 231936 | tf_op jit(solution)/shard_map/rd,kd->rk/dot_general | solution.py:101
  23.4 2.1 fusion.185
  25.5 2.1 fusion.187
  27.6 2.1 fusion.189
  29.7 2.1 fusion.191
  31.8 2.1 fusion.193
  33.9 0.7 fusion.195
  34.7 47.4 %all-gather.3.cloned.1.call-done = bf16[8192,256]{1,0:T(8,128)(2,1)} async-done(((bf16[1024,256]{1,0:T(8,128)(2,1)}), bf16[8192,256]{1,0:T(8,128)(2,1)}) %all-gather.3.cloned.1.call-update) | async-done | bytes 4194320 | tf_op jit(solution)/shard_map/all_gather | solution.py:56
  82.1 6.9 %reshape.304 = bf16[64,128,2,128]{3,2,1,0:T(2,128)(2,1)} reshape(bf16[8192,256]{1,0:T(8,128)(2,1)} %all-gather.3.cloned.1.call-done) | data formatting | bytes 8388608 | tf_op jit(solution)/shard_map/reshape | solution.py:60
  89.0 6.8 %fusion.12 = bf16[2,16,128,128]{3,1,2,0:T(8,128)(2,1)S(1)} fusion(bf16[64,128,2,128]{3,2,1,0:T(2,128)(2,1)} %reshape.304, pred[2,16,64]{2,1,0:T(8,128)(4,1)S(1)} %and.111, pred[16,64]{1,0:T(8,128)(4,1)S(1)} %and.113), kind=kOutput, calls=%fused_computation.21 | convolution fusion | flops 67635200 | bytes 5245952 | tf_op jit(solution)/shard_map/hsb,bthd->hstd/dot_general | solution.py:62
  96.1 1.0 fusion.180
  97.1 0.9 fusion.182
  98.1 57.9 %all-gather.5.cloned.1.call-done = bf16[8192,256]{1,0:T(8,128)(2,1)} async-done(((bf16[1024,256]{1,0:T(8,128)(2,1)}), bf16[8192,256]{1,0:T(8,128)(2,1)}) %all-gather.5.cloned.1.call-update) | async-done | bytes 4194320 | tf_op jit(solution)/shard_map/all_gather | solution.py:57
  155.9 6.9 %reshape.305 = bf16[64,128,2,128]{3,2,1,0:T(2,128)(2,1)} reshape(bf16[8192,256]{1,0:T(8,128)(2,1)} %all-gather.5.cloned.1.call-done) | data formatting | bytes 8388608 | tf_op jit(solution)/shard_map/reshape | solution.py:61
  162.9 6.8 %fusion.15 = bf16[2,16,128,128]{3,1,2,0:T(8,128)(2,1)S(1)} fusion(bf16[64,128,2,128]{3,2,1,0:T(2,128)(2,1)} %reshape.305, pred[2,16,64]{2,1,0:T(8,128)(4,1)S(1)} %and.111, pred[16,64]{1,0:T(8,128)(4,1)S(1)} %and.113), kind=kOutput, calls=%fused_computation.22 | convolution fusion | flops 67635200 | bytes 5245952 | tf_op jit(solution)/shard_map/hsb,bthd->hstd/dot_general | solution.py:65
  181.6 2.3 %convolution_convert_fusion = bf16[128,4096]{1,0:T(8,128)(2,1)} fusion(bf16[128,1024]{0,1:T(8,128)(2,1)S(1)} %fusion.57, bf16[1024,4096]{1,0:T(8,128)(2,1)S(1)} %bitcast.72), kind=kOutput, calls=%fused_computation | convolution fusion | flops 1074266112 | bytes 9699328 | tf_op jit(solution)/shard_map/dot_general | solution.py:126
  183.9 25.4 %reduce-scatter.2.cloned.1.call-done = bf16[32,4096]{1,0:T(8,128)(2,1)} async-done(((bf16[128,4096]{1,0:T(8,128)(2,1)}), bf16[32,4096]{1,0:T(8,128)(2,1)}) %reduce-scatter.2.cloned.1.call-update) | async-done | bytes 262160 | tf_op jit(solution)/shard_map/reduce_scatter | solution.py:125
  (136 shorter events, 14.8 us)
Async XLA Ops:
  6.5 27.4 %copy-start = (bf16[128,1024]{1,0:T(8,128)(2,1)S(1)}, bf16[128,1024]{1,0:T(8,128)(2,1)}, u32[]{:S(2)}) copy-start(bf16[128,1024]{1,0:T(8,128)(2,1)} %param.8) | copy-start | bytes 786436
  6.5 75.6 %all-gather.3.cloned.1.call-start = ((), (), s32[]{:S(2)}) async-start(), calls=%async_computation.1 | async-start | bytes 4718592 | tf_op jit(solution)/shard_map/all_gather | solution.py:56
  7.3 148.7 %all-gather.5.cloned.1.call-start = ((), (), s32[]{:S(2)}) async-start(), calls=%async_computation.2 | async-start | bytes 4718592 | tf_op jit(solution)/shard_map/all_gather | solution.py:57
  8.0 201.3 %reduce-scatter.2.cloned.1.call-start = ((), (), s32[]{:S(2)}) async-start(), calls=%async_computation.3 | async-start | bytes 1310720 | tf_op jit(solution)/shard_map/reduce_scatter | solution.py:125
  8.1 9.3 %collective-permute-start = (bf16[128,256]{1,0:T(8,128)(2,1)}, bf16[128,256]{1,0:T(8,128)(2,1)S(1)}, u32[]{:S(2)}, u32[]{:S(2)}) collective-permute-start(bf16[128,256]{1,0:T(8,128)(2,1)} %param.9), channel_id=1, source_target_pairs={{0,4},{4,8},{8,12},{12,16},{16,20},{20,24},{24,28},{1,5},{5,9},{9,... | collective-permute-start | bytes 196616 | tf_op jit(solution)/shard_map/ppermute | solution.py:15
  11.2 7.0 %collective-permute-start.1 = (bf16[128,256]{1,0:T(8,128)(2,1)}, bf16[128,256]{1,0:T(8,128)(2,1)S(1)}, u32[]{:S(2)}, u32[]{:S(2)}) collective-permute-start(bf16[128,256]{1,0:T(8,128)(2,1)} %param.10), channel_id=1, source_target_pairs={{0,4},{4,8},{8,12},{12,16},{16,20},{20,24},{24,28},{1,5},{5,9},{9,... | collective-permute-start | bytes 196616 | tf_op jit(solution)/shard_map/ppermute | solution.py:15
  19.1 12.7 %copy-start.8 = (bf16[256,256]{1,0:T(8,128)(2,1)}, bf16[256,256]{1,0:T(8,128)(2,1)S(1)}, u32[]{:S(2)}) copy-start(bf16[256,256]{1,0:T(8,128)(2,1)S(1)} %constant_dynamic-update-slice_fusion.2) | copy-start | bytes 393220
  162.9 7.2 %copy-start.11 = (f32[128]{0:T(128)S(1)}, f32[128]{0:T(128)}, u32[]{:S(2)}) copy-start(f32[128]{0:T(128)} %get-tuple-element.11) | copy-start | bytes 1540
  162.9 7.2 %copy-start.19 = (f32[128]{0:T(128)S(1)}, f32[128]{0:T(128)}, u32[]{:S(2)}) copy-start(f32[128]{0:T(128)} %get-tuple-element.13) | copy-start | bytes 1540
  169.8 2.1 copy-start.17
  170.8 2.3 %copy-start.16 = (f32[128]{0:T(128)S(1)}, f32[128]{0:T(128)}, u32[]{:S(2)}) copy-start(f32[128]{0:T(128)} %get-tuple-element.25) | copy-start | bytes 1540
  173.1 1.9 copy-start.15
  174.8 2.1 copy-start.13
  175.7 2.6 %copy-start.12 = (f32[128]{0:T(128)S(1)}, f32[128]{0:T(128)}, u32[]{:S(2)}) copy-start(f32[128]{0:T(128)} %get-tuple-element.41) | copy-start | bytes 1540
  175.7 5.8 %slice-start = ((s8[8388608]{0:T(1024)(128)(4,1)}), s8[4194304]{0:T(1024)(128)(4,1)S(1)}, s32[]{:S(2)}) async-start(s8[8388608]{0:T(1024)(128)(4,1)} %bitcast.71), calls=%async_computation.4 | async-start | bytes 8388608
  176.4 2.6 %copy-start.7 = (f32[128,256]{0,1:T(8,128)S(1)}, f32[128,256]{0,1:T(8,128)}, u32[]{:S(2)}) copy-start(f32[128,256]{0,1:T(8,128)} %get-tuple-element.14) | copy-start | bytes 393220
  176.4 2.7 %copy-start.6 = (f32[128,256]{0,1:T(8,128)S(1)}, f32[128,256]{0,1:T(8,128)}, u32[]{:S(2)}) copy-start(f32[128,256]{0,1:T(8,128)} %get-tuple-element.18) | copy-start | bytes 393220
  176.4 2.7 %copy-start.5 = (f32[128,256]{0,1:T(8,128)S(1)}, f32[128,256]{0,1:T(8,128)}, u32[]{:S(2)}) copy-start(f32[128,256]{0,1:T(8,128)} %get-tuple-element.22) | copy-start | bytes 393220
  176.5 2.8 %copy-start.4 = (f32[128,256]{0,1:T(8,128)S(1)}, f32[128,256]{0,1:T(8,128)}, u32[]{:S(2)}) copy-start(f32[128,256]{0,1:T(8,128)} %get-tuple-element.26) | copy-start | bytes 393220
  176.5 2.8 %copy-start.3 = (f32[128,256]{0,1:T(8,128)S(1)}, f32[128,256]{0,1:T(8,128)}, u32[]{:S(2)}) copy-start(f32[128,256]{0,1:T(8,128)} %get-tuple-element.30) | copy-start | bytes 393220
  176.9 2.4 %copy-start.2 = (f32[128,256]{0,1:T(8,128)S(1)}, f32[128,256]{0,1:T(8,128)}, u32[]{:S(2)}) copy-start(f32[128,256]{0,1:T(8,128)} %get-tuple-element.34) | copy-start | bytes 393220
  176.9 2.5 %copy-start.1 = (f32[128,256]{0,1:T(8,128)S(1)}, f32[128,256]{0,1:T(8,128)}, u32[]{:S(2)}) copy-start(f32[128,256]{0,1:T(8,128)} %get-tuple-element.38) | copy-start | bytes 393220
  176.9 2.7 %copy-start.9 = (bf16[256,256]{1,0:T(8,128)(2,1)S(1)}, bf16[256,256]{1,0:T(8,128)(2,1)}, u32[]{:S(2)}) copy-start(bf16[256,256]{1,0:T(8,128)(2,1)} %copy-done.8) | copy-start | bytes 393220
  177.7 3.9 %slice-start.1 = ((s8[8388608]{0:T(1024)(128)(4,1)}), s8[4194304]{0:T(1024)(128)(4,1)S(1)}, s32[]{:S(2)}) async-start(s8[8388608]{0:T(1024)(128)(4,1)} %bitcast.71), calls=%async_computation.5 | async-start | bytes 8388608
  (3 other events, 4.1 us)
Sparse Core Ops, SparseCore 0:
  9.5 72.5 all-gather.2
  84.2 71.6 all-gather.4
  184.0 25.2 reduce-scatter.1
where the time goes:
time: 218 us; the launch traced here: 216 us
  waiting for transfers between devices  132 us (61%)
  matrix products  41.2 us (19%)
  local copies, waits for them, and re-layouts  17.5 us (8%)
  between operations  13.7 us (6%)
  starting transfers between devices  6.38 us (3%)
  other arithmetic  4.93 us (2%)
    all_gather x1, waiting for transfers between devices, shards(): lax.all_gather(cache_values, 'ctx', axis=0, tiled=True)  57.9 us
    all_gather x1, waiting for transfers between devices, shards(): lax.all_gather(cache_keys, 'ctx', axis=0, tiled=True)  47.4 us
    reduce_scatter x1, waiting for transfers between devices, shards(): lax.psum_scatter(jnp.dot(attention, out_weight, preferred_element_type=jn...  25.4 us
    dot_general x8, matrix products, shards(): jnp.einsum('rd,kd->rk', query_head, stretch_keyhead, preferred_element_ty...  15.5 us
    reshape x1, local copies, waits for them, and re-layouts, shards(): piece_keys = pieces[0].reshape(piece_blocks, BLOCK, kv_local, HD)  6.93 us
    reshape x1, local copies, waits for them, and re-layouts, shards(): piece_values = pieces[1].reshape(piece_blocks, BLOCK, kv_local, HD)  6.92 us
    dot_general x1, matrix products, shards(): jnp.einsum('hsb,bthd->hstd', pick_global, piece_values, preferred_element...  6.79 us
    dot_general x1, matrix products, shards(): jnp.einsum('hsb,bthd->hstd', pick_global, piece_keys, preferred_element_t...  6.78 us
  transfers between devices with their start and end apart: 5, of which 3 were waited for; matrix products, arithmetic and copies ran while one was open for 17% of the time, Pallas kernels for 0%

commit v1 on v0

v1 whole, which is shorter than its diff:
```python
import functools

import jax
import jax.numpy as jnp
from jax import lax
from jax.experimental import pallas as pl
from jax.experimental.pallas import tpu as pltpu
from jax.sharding import PartitionSpec as P

HD = 128
BLOCK = 128
CAP = 2
CB_DEV = 8
GROUPS = 2
PARTS = 4
NEG = -1e30
EXP2_SCALE = HD**-0.5 * 1.4426950408889634
F32 = jnp.float32
BF16 = jnp.bfloat16


def remote(src, dst, send_sem, recv_sem, device):
    return pltpu.make_async_remote_copy(
        src_ref=src,
        dst_ref=dst,
        send_sem=send_sem,
        recv_sem=recv_sem,
        device_id=device,
        device_id_type=pl.DeviceIdType.MESH,
    )


def kernel(
    n, n_head, kvh, group,
    list_ref, count_ref, q_ref, kn_ref, vn_ref, ck_ref, cv_ref, w_hbm,
    out_ref,
    table, meta, meta_s, far_table, far_q, prev, qstack, sendb, recvb, acc, stat,
    part_out, part_in, stat_in, att, w_v, proj, proj16, r1, s2, r2,
    meta_ss, meta_rs, smem_s, kv_ss, kv_rs, prev_ss, prev_rs, far_ss, far_rs,
    back_ss, back_rs, w_sem, p1_ss, p1_rs, p2_ss, p2_rs,
):
    me = lax.axis_index("ctx")
    hi = lax.axis_index("head")
    half = n // GROUPS
    mypos = lax.rem(me, half)
    base = me - mypos
    mirror = lax.rem(me + half, n)
    cols = w_v.shape[2]

    def w_copy(c):
        return pltpu.make_async_copy(
            w_hbm.at[:, pl.ds(c * cols, cols)], w_v.at[c], w_sem.at[c]
        )

    barrier = pltpu.get_barrier_semaphore()
    for k in range(1, n):
        pl.semaphore_signal(
            barrier, inc=1, device_id={"ctx": lax.rem(me + k, n)},
            device_id_type=pl.DeviceIdType.MESH,
        )
    for k in range(1, n_head):
        pl.semaphore_signal(
            barrier, inc=1, device_id={"head": lax.rem(hi + k, n_head)},
            device_id_type=pl.DeviceIdType.MESH,
        )

    blk = list_ref[...]
    lane = lax.broadcasted_iota(jnp.int32, blk.shape, 1)
    used = jnp.where(lane < count_ref[...], blk, -1)
    for o in range(n):
        mine = (used >= o * CB_DEV) & (used < (o + 1) * CB_DEV)
        first = jnp.min(jnp.where(mine, used - o * CB_DEV, CB_DEV - 1), axis=1, keepdims=True)
        last = jnp.max(jnp.where(mine, used - o * CB_DEV, 0), axis=1, keepdims=True)
        two = (last > first).astype(jnp.int32)
        table[o, 0:kvh, :] = jnp.broadcast_to(first, (kvh, 128))
        table[o, kvh : 2 * kvh, :] = jnp.broadcast_to(last, (kvh, 128))
        table[o, 2 * kvh : 3 * kvh, :] = jnp.broadcast_to(two, (kvh, 128))

    pl.semaphore_wait(barrier, n - 1 + n_head - 1)

    def meta_send(k):
        d = lax.rem(me + k, n)
        return remote(table.at[d], meta.at[me], meta_ss.at[k], meta_rs.at[me], {"ctx": d})

    def meta_recv(d):
        return remote(table.at[d], meta.at[d], meta_ss.at[0], meta_rs.at[d], {"ctx": mirror})

    for k in range(1, n):
        meta_send(k).start()
    far_copies = []
    if GROUPS == 2:
        far_copies = [
            remote(table, far_table, far_ss.at[0], far_rs.at[0], {"ctx": mirror}),
            remote(q_ref, far_q, far_ss.at[1], far_rs.at[1], {"ctx": mirror}),
        ]
    for copy in far_copies:
        copy.start()
    nxt = lax.rem(me + 1, n)
    prev_copies = [
        remote(kn_ref, prev.at[0], prev_ss.at[0], prev_rs.at[0], {"ctx": nxt}),
        remote(vn_ref, prev.at[1], prev_ss.at[1], prev_rs.at[1], {"ctx": nxt}),
    ]

    def own_smem():
        return pltpu.make_async_copy(table.at[me], meta_s.at[me], smem_s.at[me])

    own_smem().start()

    def smem_copy(d):
        return pltpu.make_async_copy(meta.at[d], meta_s.at[d], smem_s.at[d])

    def target(x, k):
        pi = lax.rem(mypos + k, half)
        p = base + pi
        d = p if x == 0 else lax.rem(p + half, n)
        return pi, p, d

    def gather(d, dst):
        for h in range(kvh):
            for s in range(CAP):
                index = meta_s[d, s * kvh + h, 0]
                cut = slice(h * HD, (h + 1) * HD)
                dst[h, 0, s * BLOCK : (s + 1) * BLOCK, :] = ck_ref[index, :, cut]
                dst[h, 1, s * BLOCK : (s + 1) * BLOCK, :] = cv_ref[index, :, cut]

    def kv_send(x, k):
        pi, p, _ = target(x, k)
        return remote(
            sendb.at[x, pi], recvb.at[x, mypos], kv_ss.at[x, pi], kv_rs.at[x, mypos], {"ctx": p}
        )

    def kv_recv(x, k):
        pi, p, _ = target(x, half - k)
        return pi, remote(
            sendb.at[x, pi], recvb.at[x, pi], kv_ss.at[x, pi], kv_rs.at[x, pi], {"ctx": p}
        )

    order = list(range(GROUPS))[::-1]
    for x in order:
        def fetch(k, _, x=x):
            _, _, d = target(x, k)
            meta_recv(d).wait_recv()
            smem_copy(d).start()
            return 0

        lax.fori_loop(1, half, fetch, 0)
    if GROUPS == 2:
        meta_recv(mirror).wait_recv()
        smem_copy(mirror).start()
    for x in order:
        def give(k, _, x=x):
            pi, _, d = target(x, k)
            smem_copy(d).wait()
            gather(d, sendb.at[x, pi])
            kv_send(x, k).start()
            return 0

        lax.fori_loop(1, half, give, 0)
        if x == order[0]:
            for copy in prev_copies:
                @pl.when(me < n - 1)
                def _(copy=copy):
                    copy.start()

    for copy_c in range(PARTS):
        w_copy(copy_c).start()
    own_smem().wait()
    gather(me, recvb.at[0, mypos])
    if GROUPS == 2:
        smem_copy(mirror).wait()
        gather(mirror, recvb.at[1, mypos])

    width = group * BLOCK

    def stack(x, ref):
        for h in range(kvh):
            for j in range(group):
                column = (h * group + j) * HD
                qstack[x, h, j * BLOCK : (j + 1) * BLOCK, :] = ref[:, column : column + HD]

    def attend(x, h, keys, values, mask):
        scores = lax.dot_general(
            keys, qstack[x, h], (((1,), (1,)), ((), ())), preferred_element_type=F32
        )
        scores = mask(scores)
        old_max = stat[x, h : h + 1, :]
        new_max = jnp.maximum(old_max, jnp.max(scores, axis=0, keepdims=True))
        weights = jnp.exp2((scores - new_max) * EXP2_SCALE)
        fade = jnp.exp2((old_max - new_max) * EXP2_SCALE)
        total = stat[x, kvh + h : kvh + h + 1, :] * fade
        stat[x, h : h + 1, :] = new_max
        stat[x, kvh + h : kvh + h + 1, :] = total + jnp.sum(weights, axis=0, keepdims=True)
        mixture = lax.dot_general(
            values, weights.astype(BF16), (((0,), (0,)), ((), ())), preferred_element_type=F32
        )
        acc[x, h] = acc[x, h] * fade + mixture

    def attend_cache(x, pi):
        flags = table if x == 0 else far_table
        for h in range(kvh):
            two = flags[base + pi, 2 * kvh + h : 2 * kvh + h + 1, :]
            two = jnp.concatenate([two] * group, axis=1)

            def mask(scores):
                return jnp.concatenate(
                    [scores[:BLOCK], jnp.where(two > 0, scores[BLOCK:], NEG)], axis=0
                )

            attend(x, h, recvb[x, pi, h, 0], recvb[x, pi, h, 1], mask)

    def attend_arrivals(x):
        def step(k, _):
            pi, copy = kv_recv(x, k)
            copy.wait_recv()
            attend_cache(x, pi)
            return 0

        lax.fori_loop(1, half, step, 0)

    stat[:, 0:kvh, :] = jnp.full((GROUPS, kvh, width), NEG, F32)
    stat[:, kvh:, :] = jnp.zeros((GROUPS, stat.shape[1] - kvh, width), F32)
    acc[...] = jnp.zeros_like(acc)
    stack(0, q_ref)

    def causal(scores):
        key = lax.broadcasted_iota(jnp.int32, scores.shape, 0)
        row = lax.broadcasted_iota(jnp.int32, scores.shape, 1) & (BLOCK - 1)
        return jnp.where(key <= row, scores, NEG)

    for h in range(kvh):
        cut = slice(h * HD, (h + 1) * HD)
        attend(0, h, kn_ref[:, cut], vn_ref[:, cut], causal)
    attend_cache(0, mypos)

    back_copies = []
    if GROUPS == 2:
        for copy in far_copies:
            copy.wait_recv()
        stack(1, far_q)
        attend_cache(1, mypos)
        attend_arrivals(1)
        part_out[...] = acc[1].astype(BF16)
        back_copies = [
            remote(stat.at[1], stat_in, back_ss.at[0], back_rs.at[0], {"ctx": mirror}),
            remote(part_out, part_in, back_ss.at[1], back_rs.at[1], {"ctx": mirror}),
        ]
        for copy in back_copies:
            copy.start()

    @pl.when(me > 0)
    def _():
        for copy in prev_copies:
            copy.wait_recv()
        for h in range(kvh):
            cut = slice(h * HD, (h + 1) * HD)
            attend(0, h, prev[0, :, cut], prev[1, :, cut], lambda scores: scores)

    attend_arrivals(0)
    for copy in back_copies:
        copy.wait_recv()
    for h in range(kvh):
        own = acc[0, h]
        total = stat[0, kvh + h : kvh + h + 1, :]
        if GROUPS == 2:
            here, there = stat[0, h : h + 1, :], stat_in[h : h + 1, :]
            top = jnp.maximum(here, there)
            fade_here = jnp.exp2((here - top) * EXP2_SCALE)
            fade_there = jnp.exp2((there - top) * EXP2_SCALE)
            own = own * fade_here + part_in[h].astype(F32) * fade_there
            total = total * fade_here + stat_in[kvh + h : kvh + h + 1, :] * fade_there
        own = own / total
        for j in range(group):
            column = (h * group + j) * HD
            block = own[:, j * BLOCK : (j + 1) * BLOCK]
            att[:, column : column + HD] = block.T.astype(BF16)

    core = lax.rem(hi, 2)
    row = hi // 2
    core_peer = hi + 1 - 2 * core
    row_peer = lax.rem(hi + 2, n_head)
    piece = BLOCK // n_head

    def to_core(c):
        return remote(
            proj16.at[c, 1 - core], r1.at[c], p1_ss.at[c], p1_rs.at[c], {"head": core_peer}
        )

    def to_row(c):
        return remote(s2.at[c], r2.at[c], p2_ss.at[c], p2_rs.at[c], {"head": row_peer})

    def forward(c):
        to_core(c).wait_recv()
        s2[c] = (proj[c, core, 1 - row] + r1[c, 1 - row].astype(F32)).astype(BF16)
        to_row(c).start()

    for c in range(PARTS):
        w_copy(c).wait()
        product = jnp.dot(att[...], w_v[c], preferred_element_type=F32)
        for i in range(n_head):
            rows = product[i * piece : (i + 1) * piece]
            proj[c, i % 2, i // 2] = rows
            proj16[c, i % 2, i // 2] = rows.astype(BF16)
        to_core(c).start()
        if c > 0:
            forward(c - 1)
    forward(PARTS - 1)
    for c in range(PARTS):
        to_row(c).wait_recv()
        out_ref[:, c * cols : (c + 1) * cols] = (
            proj[c, core, row] + r1[c, row].astype(F32) + r2[c].astype(F32)
        ).astype(BF16)

    for k in range(1, n):
        meta_send(k).wait_send()
    for copy in far_copies + back_copies:
        copy.wait_send()
    for copy in prev_copies:
        @pl.when(me < n - 1)
        def _(copy=copy):
            copy.wait_send()
    for x in range(GROUPS):
        def sent(k, _, x=x):
            kv_send(x, k).wait_send()
            return 0

        lax.fori_loop(1, half, sent, 0)
    for c in range(PARTS):
        to_core(c).wait_send()
        to_row(c).wait_send()


def shards(
    queries, keys_new, values_new, cache_keys, cache_values, block_list, block_count, out_weight
):
    n = lax.axis_size("ctx")
    n_head = lax.axis_size("head")
    kvh = keys_new.shape[1] // HD
    group = queries.shape[1] // keys_new.shape[1]
    half = n // GROUPS
    width = group * BLOCK
    d_in, d_out = out_weight.shape
    cols = d_out // PARTS
    piece = BLOCK // n_head
    vmem, any_space = pl.BlockSpec(memory_space=pltpu.VMEM), pl.BlockSpec(memory_space=pl.ANY)
    dma = pltpu.SemaphoreType.DMA
    keys_slot = CAP * BLOCK
    scratch = [
        pltpu.VMEM((n, 8, 128), jnp.int32),
        pltpu.VMEM((n, 8, 128), jnp.int32),
        pltpu.SMEM((n, 8, 128), jnp.int32),
        pltpu.VMEM((n, 8, 128), jnp.int32),
        pltpu.VMEM(queries.shape, BF16),
        pltpu.VMEM((2,) + keys_new.shape, BF16),
        pltpu.VMEM((GROUPS, kvh, width, HD), BF16),
        pltpu.VMEM((GROUPS, half, kvh, 2, keys_slot, HD), BF16),
        pltpu.VMEM((GROUPS, half, kvh, 2, keys_slot, HD), BF16),
        pltpu.VMEM((GROUPS, kvh, HD, width), F32),
        pltpu.VMEM((GROUPS, 8, width), F32),
        pltpu.VMEM((kvh, HD, width), BF16),
        pltpu.VMEM((kvh, HD, width), BF16),
        pltpu.VMEM((8, width), F32),
        pltpu.VMEM((BLOCK, d_in), BF16),
        pltpu.VMEM((PARTS, d_in, cols), BF16),
        pltpu.VMEM((PARTS, 2, n_head // 2, piece, cols), F32),
        pltpu.VMEM((PARTS, 2, n_head // 2, piece, cols), BF16),
        pltpu.VMEM((PARTS, n_head // 2, piece, cols), BF16),
        pltpu.VMEM((PARTS, piece, cols), BF16),
        pltpu.VMEM((PARTS, piece, cols), BF16),
        dma((n,)), dma((n,)), dma((n,)),
        dma((GROUPS, half)), dma((GROUPS, half)),
        dma((2,)), dma((2,)), dma((2,)), dma((2,)), dma((2,)), dma((2,)),
        dma((PARTS,)), dma((PARTS,)), dma((PARTS,)), dma((PARTS,)), dma((PARTS,)),
    ]
    return pl.pallas_call(
        functools.partial(kernel, n, n_head, kvh, group),
        out_shape=jax.ShapeDtypeStruct((piece, d_out), BF16),
        in_specs=[vmem] * 7 + [any_space],
        out_specs=vmem,
        scratch_shapes=scratch,
        compiler_params=pltpu.CompilerParams(
            collective_id=0, has_side_effects=True, vmem_limit_bytes=56 * 2**20
        ),
    )(
        block_list.reshape(kvh, -1), block_count.reshape(kvh, 1),
        queries, keys_new, values_new,
        cache_keys.reshape(CB_DEV, BLOCK, -1), cache_values.reshape(CB_DEV, BLOCK, -1), out_weight,
    )


def solution(mesh):
    return jax.shard_map(
        shards,
        mesh=mesh,
        in_specs=(
            P("ctx", "head"),
            P("ctx", "head"),
            P("ctx", "head"),
            P("ctx", "head"),
            P("ctx", "head"),
            P("head", "ctx", None),
            P("head", "ctx"),
            P("head", None),
        ),
        out_specs=P(("ctx", "head"), None),
        check_vma=False,
    )
```

time: 218 us -> 64.1 us (0.29)
  waiting for transfers between devices: 132 us -> 0 us
  Pallas kernels: 0 us -> 61 us
  matrix products: 41.2 us -> 0 us
  local copies, waits for them, and re-layouts: 17.5 us -> 2.97 us
  between operations: 13.7 us -> 0.01 us
  starting transfers between devices: 6.38 us -> 0 us
  other arithmetic: 4.93 us -> 0 us
    all_gather x2 -> x0, waiting for transfers between devices: 105 us -> none  [the longest x1 57.9 us: shards(): lax.all_gather(cache_values, 'ctx', axis=0, tiled=True)]
    pallas_call x0 -> x1, Pallas kernels: none -> 61 us  [shards(): pl.pallas_call(functools.partial(kernel, n, n_head, kvh, group), out_shap...]
    dot_general x35 -> x0, matrix products: 41.2 us -> none  [the longest x8 15.5 us: shards(): jnp.einsum('rd,kd->rk', query_head, stretch_keyhead, preferred_element_ty...]
    reduce_scatter x1 -> x0, waiting for transfers between devices: 25.4 us -> none  [shards(): lax.psum_scatter(jnp.dot(attention, out_weight, preferred_element_type=jn...]
    reshape x2 -> x0, local copies, waits for them, and re-layouts: 13.9 us -> none  [the longest x1 6.93 us: shards(): piece_keys = pieces[0].reshape(piece_blocks, BLOCK, kv_local, HD)]
    ppermute x2 -> x0, starting transfers between devices: 6.3 us -> none  [passed_along(): return lax.ppermute(shard, axis, pairs)]
    unnamed x46 -> x2, local copies, waits for them, and re-layouts: 0.1 us -> 2.97 us
    reduce_sum x16 -> x0, other arithmetic: 2.81 us -> none  [the longest x8 2.35 us: shards(): jnp.sum(cache_weights, axis=1) + jnp.sum(stretch_weights, axis=1)]
  transfers between devices with their start and end apart: 5 -> 0, of which waited for: 3 -> 0; matrix products, arithmetic and copies ran while one was open for 17% -> 0% of each run, Pallas kernels for 0% -> 0%
where the time goes in v1:
time: 64.1 us; the launch traced here: 63.9 us
  Pallas kernels  61 us (95%)
  local copies, waits for them, and re-layouts  2.97 us (5%)
    pallas_call x1, Pallas kernels, shards(): pl.pallas_call(functools.partial(kernel, n, n_head, kvh, group), out_shap...  61 us
    unnamed x2, local copies, waits for them, and re-layouts  2.97 us

profile of v1, /device:TPU:3, one launch (start us, length us, event | category | flops | bytes accessed | tf_op | source)
XLA Modules:
  0.0 63.9 jit_solution(4559481520486098055)
XLA Ops:
  0.0 1.3 %copy.9.count_ref = s32[2,1]{1,0:T(2,128)} copy(s32[2,1]{0,1:T(1,128)} %param.14) | data formatting | bytes 16 | tf_op args[6]
  1.3 61.0 %shard_map.82 = bf16[32,4096]{1,0:T(8,128)(2,1)} custom-call(s32[2,16]{1,0:T(2,128)} %bitcast.5, s32[2,1]{1,0:T(2,128)} %copy.9.count_ref, bf16[128,1024]{1,0:T(8,128)(2,1)} %q_ref.1, bf16[128,256]{1,0:T(8,128)(2,1)} %kn_ref.1, bf16[128,256]{1,0:T(8,128)(2,1)} %vn_ref.1, bf16[8,128,256]{2,1,0:T(8,128)(2,1)} %bitcast.3, bf16[8,128,256]{2,1,0:T(8,128)(2,1)} %bitcast.4, ...), custom_call_target="tpu_custom_call" | custom-call | tf_op jit(solution)/shard_map/pallas_call | solution.py:374
  62.3 1.7 %copy.11 = bf16[32,4096]{1,0:T(8,128)(2,1)} copy(bf16[32,4096]{1,0:T(8,128)(2,1)} %shard_map.82) | data formatting | bytes 524288

commit v2 on v1

--- a/solution.py
+++ b/solution.py
@@ -66,7 +66,10 @@
 
     blk = list_ref[...]
     lane = lax.broadcasted_iota(jnp.int32, blk.shape, 1)
-    used = jnp.where(lane < count_ref[...], blk, -1)
+    head = lax.broadcasted_iota(jnp.int32, blk.shape, 0)
+    used = jnp.full_like(blk, -1)
+    for h in range(kvh):
+        used = jnp.where((head == h) & (lane < count_ref[0, h]), blk, used)
     for o in range(n):
         mine = (used >= o * CB_DEV) & (used < (o + 1) * CB_DEV)
         first = jnp.min(jnp.where(mine, used - o * CB_DEV, CB_DEV - 1), axis=1, keepdims=True)
@@ -109,8 +112,16 @@
     def smem_copy(d):
         return pltpu.make_async_copy(meta.at[d], meta_s.at[d], smem_s.at[d])
 
+    def partner(k):
+        place, total = 1, 0
+        while place < half:
+            a, b = lax.rem(mypos // place, 2), lax.rem(k // place, 2)
+            total = total + place * (a + b - 2 * a * b)
+            place *= 2
+        return total
+
     def target(x, k):
-        pi = lax.rem(mypos + k, half)
+        pi = partner(k)
         p = base + pi
         d = p if x == 0 else lax.rem(p + half, n)
         return pi, p, d
@@ -130,7 +141,7 @@
         )
 
     def kv_recv(x, k):
-        pi, p, _ = target(x, half - k)
+        pi, p, _ = target(x, k)
         return pi, remote(
             sendb.at[x, pi], recvb.at[x, pi], kv_ss.at[x, pi], kv_rs.at[x, pi], {"ctx": p}
         )
@@ -152,15 +163,11 @@
             pi, _, d = target(x, k)
             smem_copy(d).wait()
             gather(d, sendb.at[x, pi])
-            kv_send(x, k).start()
+            if x == order[0]:
+                kv_send(x, k).start()
             return 0
 
         lax.fori_loop(1, half, give, 0)
-        if x == order[0]:
-            for copy in prev_copies:
-                @pl.when(me < n - 1)
-                def _(copy=copy):
-                    copy.start()
 
     for copy_c in range(PARTS):
         w_copy(copy_c).start()
@@ -213,6 +220,9 @@
             pi, copy = kv_recv(x, k)
             copy.wait_recv()
             attend_cache(x, pi)
+            if x != order[-1]:
+                kv_send(x, k).wait_send()
+                kv_send(x - 1, k).start()
             return 0
 
         lax.fori_loop(1, half, step, 0)
@@ -245,6 +255,10 @@
             remote(part_out, part_in, back_ss.at[1], back_rs.at[1], {"ctx": mirror}),
         ]
         for copy in back_copies:
+            copy.start()
+    for copy in prev_copies:
+        @pl.when(me < n - 1)
+        def _(copy=copy):
             copy.start()
 
     @pl.when(me > 0)
@@ -318,12 +332,11 @@
         @pl.when(me < n - 1)
         def _(copy=copy):
             copy.wait_send()
-    for x in range(GROUPS):
-        def sent(k, _, x=x):
-            kv_send(x, k).wait_send()
-            return 0
-
-        lax.fori_loop(1, half, sent, 0)
+    def sent(k, _):
+        kv_send(0, k).wait_send()
+        return 0
+
+    lax.fori_loop(1, half, sent, 0)
     for c in range(PARTS):
         to_core(c).wait_send()
         to_row(c).wait_send()
@@ -342,6 +355,7 @@
     cols = d_out // PARTS
     piece = BLOCK // n_head
     vmem, any_space = pl.BlockSpec(memory_space=pltpu.VMEM), pl.BlockSpec(memory_space=pl.ANY)
+    smem = pl.BlockSpec(memory_space=pltpu.SMEM)
     dma = pltpu.SemaphoreType.DMA
     keys_slot = CAP * BLOCK
     scratch = [
@@ -374,14 +388,14 @@
     return pl.pallas_call(
         functools.partial(kernel, n, n_head, kvh, group),
         out_shape=jax.ShapeDtypeStruct((piece, d_out), BF16),
-        in_specs=[vmem] * 7 + [any_space],
+        in_specs=[vmem, smem] + [vmem] * 5 + [any_space],
         out_specs=vmem,
         scratch_shapes=scratch,
         compiler_params=pltpu.CompilerParams(
             collective_id=0, has_side_effects=True, vmem_limit_bytes=56 * 2**20
         ),
     )(
-        block_list.reshape(kvh, -1), block_count.reshape(kvh, 1),
+        block_list.reshape(kvh, -1), block_count.reshape(1, kvh),
         queries, keys_new, values_new,
         cache_keys.reshape(CB_DEV, BLOCK, -1), cache_values.reshape(CB_DEV, BLOCK, -1), out_weight,
     )

time: 64.1 us -> 67.5 us (1.053)
  the two profiles are of different devices: /device:TPU:3 before, /device:TPU:9 now
where the time goes in v2:
time: 67.5 us; the launch traced here: 67.3 us
  Pallas kernels  65.6 us (97%)
  local copies, waits for them, and re-layouts  1.67 us (2%)
    pallas_call x1, Pallas kernels, shards(): pl.pallas_call(functools.partial(kernel, n, n_head, kvh, group), out_shap...  65.6 us
    unnamed x1, local copies, waits for them, and re-layouts  1.67 us

profile of v2, /device:TPU:9, one launch (start us, length us, event | category | flops | bytes accessed | tf_op | source)
XLA Modules:
  0.0 67.3 jit_solution(10458735328396218894)
XLA Ops:
  0.0 65.6 %shard_map.82 = bf16[32,4096]{1,0:T(8,128)(2,1)} custom-call(s32[2,16]{1,0:T(2,128)} %bitcast.6, s32[1,2]{1,0:T(1,128)} %bitcast.7, bf16[128,1024]{1,0:T(8,128)(2,1)} %q_ref.1, bf16[128,256]{1,0:T(8,128)(2,1)} %kn_ref.1, bf16[128,256]{1,0:T(8,128)(2,1)} %vn_ref.1, bf16[8,128,256]{2,1,0:T(8,128)(2,1)} %bitcast.4, bf16[8,128,256]{2,1,0:T(8,128)(2,1)} %bitcast.5, ...), custom_call_target="tpu_custom_call" | custom-call | tf_op jit(solution)/shard_map/pallas_call | solution.py:388
  65.6 1.7 %copy.10 = bf16[32,4096]{1,0:T(8,128)(2,1)} copy(bf16[32,4096]{1,0:T(8,128)(2,1)} %shard_map.82) | data formatting | bytes 524288

commit v3 on v2

--- a/solution.py
+++ b/solution.py
@@ -121,7 +121,7 @@
         return total
 
     def target(x, k):
-        pi = partner(k)
+        pi = partner(half - k)
         p = base + pi
         d = p if x == 0 else lax.rem(p + half, n)
         return pi, p, d
@@ -202,9 +202,9 @@
         )
         acc[x, h] = acc[x, h] * fade + mixture
 
-    def attend_cache(x, pi):
+    def attend_cache(x, pi, heads=range(kvh)):
         flags = table if x == 0 else far_table
-        for h in range(kvh):
+        for h in heads:
             two = flags[base + pi, 2 * kvh + h : 2 * kvh + h + 1, :]
             two = jnp.concatenate([two] * group, axis=1)
 
@@ -215,17 +215,14 @@
 
             attend(x, h, recvb[x, pi, h, 0], recvb[x, pi, h, 1], mask)
 
-    def attend_arrivals(x):
+    def attend_arrivals(x, stop):
         def step(k, _):
             pi, copy = kv_recv(x, k)
             copy.wait_recv()
             attend_cache(x, pi)
-            if x != order[-1]:
-                kv_send(x, k).wait_send()
-                kv_send(x - 1, k).start()
             return 0
 
-        lax.fori_loop(1, half, step, 0)
+        lax.fori_loop(1, stop, step, 0)
 
     stat[:, 0:kvh, :] = jnp.full((GROUPS, kvh, width), NEG, F32)
     stat[:, kvh:, :] = jnp.zeros((GROUPS, stat.shape[1] - kvh, width), F32)
@@ -242,20 +239,32 @@
         attend(0, h, kn_ref[:, cut], vn_ref[:, cut], causal)
     attend_cache(0, mypos)
 
+    def follow(k, _):
+        kv_send(1, k).wait_send()
+        kv_send(0, k).start()
+        return 0
+
     back_copies = []
     if GROUPS == 2:
+        lax.fori_loop(1, half, follow, 0)
         for copy in far_copies:
             copy.wait_recv()
         stack(1, far_q)
         attend_cache(1, mypos)
-        attend_arrivals(1)
-        part_out[...] = acc[1].astype(BF16)
-        back_copies = [
-            remote(stat.at[1], stat_in, back_ss.at[0], back_rs.at[0], {"ctx": mirror}),
-            remote(part_out, part_in, back_ss.at[1], back_rs.at[1], {"ctx": mirror}),
-        ]
-        for copy in back_copies:
+        attend_arrivals(1, half - 1)
+        pi, copy = kv_recv(1, half - 1)
+        copy.wait_recv()
+        for h in range(kvh):
+            attend_cache(1, pi, [h])
+            part_out[h] = acc[1, h].astype(BF16)
+            copy = remote(
+                part_out.at[h], part_in.at[h], back_ss.at[h], back_rs.at[h], {"ctx": mirror}
+            )
             copy.start()
+            back_copies.append(copy)
+        copy = remote(stat.at[1], stat_in, back_ss.at[kvh], back_rs.at[kvh], {"ctx": mirror})
+        copy.start()
+        back_copies.append(copy)
     for copy in prev_copies:
         @pl.when(me < n - 1)
         def _(copy=copy):
@@ -269,7 +278,7 @@
             cut = slice(h * HD, (h + 1) * HD)
             attend(0, h, prev[0, :, cut], prev[1, :, cut], lambda scores: scores)
 
-    attend_arrivals(0)
+    attend_arrivals(0, half)
     for copy in back_copies:
         copy.wait_recv()
     for h in range(kvh):
@@ -382,7 +391,7 @@
         pltpu.VMEM((PARTS, piece, cols), BF16),
         dma((n,)), dma((n,)), dma((n,)),
         dma((GROUPS, half)), dma((GROUPS, half)),
-        dma((2,)), dma((2,)), dma((2,)), dma((2,)), dma((2,)), dma((2,)),
+        dma((2,)), dma((2,)), dma((2,)), dma((2,)), dma((kvh + 1,)), dma((kvh + 1,)),
         dma((PARTS,)), dma((PARTS,)), dma((PARTS,)), dma((PARTS,)), dma((PARTS,)),
     ]
     return pl.pallas_call(

time: 67.5 us -> 68.4 us (1.013)
  the two profiles are of different devices: /device:TPU:9 before, /device:TPU:17 now
where the time goes in v3:
time: 68.4 us; the launch traced here: 68.2 us
  Pallas kernels  66.6 us (97%)
  local copies, waits for them, and re-layouts  1.67 us (2%)
    pallas_call x1, Pallas kernels, shards(): pl.pallas_call(functools.partial(kernel, n, n_head, kvh, group), out_shap...  66.6 us
    unnamed x1, local copies, waits for them, and re-layouts  1.67 us

profile of v3, /device:TPU:17, one launch (start us, length us, event | category | flops | bytes accessed | tf_op | source)
XLA Modules:
  0.0 68.2 jit_solution(1250657468346670945)
XLA Ops:
  0.0 66.6 %shard_map.82 = bf16[32,4096]{1,0:T(8,128)(2,1)} custom-call(s32[2,16]{1,0:T(2,128)} %bitcast.6, s32[1,2]{1,0:T(1,128)} %bitcast.7, bf16[128,1024]{1,0:T(8,128)(2,1)} %q_ref.1, bf16[128,256]{1,0:T(8,128)(2,1)} %kn_ref.1, bf16[128,256]{1,0:T(8,128)(2,1)} %vn_ref.1, bf16[8,128,256]{2,1,0:T(8,128)(2,1)} %bitcast.4, bf16[8,128,256]{2,1,0:T(8,128)(2,1)} %bitcast.5, ...), custom_call_target="tpu_custom_call" | custom-call | tf_op jit(solution)/shard_map/pallas_call | solution.py:397
  66.6 1.7 %copy.10 = bf16[32,4096]{1,0:T(8,128)(2,1)} copy(bf16[32,4096]{1,0:T(8,128)(2,1)} %shard_map.82) | data formatting | bytes 524288

commit v4 on v3

--- a/solution.py
+++ b/solution.py
@@ -112,16 +112,8 @@
     def smem_copy(d):
         return pltpu.make_async_copy(meta.at[d], meta_s.at[d], smem_s.at[d])
 
-    def partner(k):
-        place, total = 1, 0
-        while place < half:
-            a, b = lax.rem(mypos // place, 2), lax.rem(k // place, 2)
-            total = total + place * (a + b - 2 * a * b)
-            place *= 2
-        return total
-
     def target(x, k):
-        pi = partner(half - k)
+        pi = lax.rem(mypos + k, half)
         p = base + pi
         d = p if x == 0 else lax.rem(p + half, n)
         return pi, p, d
@@ -141,7 +133,7 @@
         )
 
     def kv_recv(x, k):
-        pi, p, _ = target(x, k)
+        pi, p, _ = target(x, half - k)
         return pi, remote(
             sendb.at[x, pi], recvb.at[x, pi], kv_ss.at[x, pi], kv_rs.at[x, pi], {"ctx": p}
         )
@@ -163,11 +155,15 @@
             pi, _, d = target(x, k)
             smem_copy(d).wait()
             gather(d, sendb.at[x, pi])
-            if x == order[0]:
-                kv_send(x, k).start()
+            kv_send(x, k).start()
             return 0
 
         lax.fori_loop(1, half, give, 0)
+        if x == order[0]:
+            for copy in prev_copies:
+                @pl.when(me < n - 1)
+                def _(copy=copy):
+                    copy.start()
 
     for copy_c in range(PARTS):
         w_copy(copy_c).start()
@@ -239,14 +235,8 @@
         attend(0, h, kn_ref[:, cut], vn_ref[:, cut], causal)
     attend_cache(0, mypos)
 
-    def follow(k, _):
-        kv_send(1, k).wait_send()
-        kv_send(0, k).start()
-        return 0
-
     back_copies = []
     if GROUPS == 2:
-        lax.fori_loop(1, half, follow, 0)
         for copy in far_copies:
             copy.wait_recv()
         stack(1, far_q)
@@ -265,10 +255,6 @@
         copy = remote(stat.at[1], stat_in, back_ss.at[kvh], back_rs.at[kvh], {"ctx": mirror})
         copy.start()
         back_copies.append(copy)
-    for copy in prev_copies:
-        @pl.when(me < n - 1)
-        def _(copy=copy):
-            copy.start()
 
     @pl.when(me > 0)
     def _():
@@ -341,11 +327,12 @@
         @pl.when(me < n - 1)
         def _(copy=copy):
             copy.wait_send()
-    def sent(k, _):
-        kv_send(0, k).wait_send()
-        return 0
-
-    lax.fori_loop(1, half, sent, 0)
+    for x in range(GROUPS):
+        def sent(k, _, x=x):
+            kv_send(x, k).wait_send()
+            return 0
+
+        lax.fori_loop(1, half, sent, 0)
     for c in range(PARTS):
         to_core(c).wait_send()
         to_row(c).wait_send()

time: 68.4 us -> 62.9 us (0.920)
  the two profiles are of different devices: /device:TPU:17 before, /device:TPU:3 now
where the time goes in v4:
time: 62.9 us; the launch traced here: 62.7 us
  Pallas kernels  61.1 us (97%)
  local copies, waits for them, and re-layouts  1.67 us (3%)
    pallas_call x1, Pallas kernels, shards(): pl.pallas_call(functools.partial(kernel, n, n_head, kvh, group), out_shap...  61.1 us
    unnamed x1, local copies, waits for them, and re-layouts  1.67 us

profile of v4, /device:TPU:3, one launch (start us, length us, event | category | flops | bytes accessed | tf_op | source)
XLA Modules:
  0.0 62.7 jit_solution(8853224804435746184)
XLA Ops:
  0.0 61.1 %shard_map.82 = bf16[32,4096]{1,0:T(8,128)(2,1)} custom-call(s32[2,16]{1,0:T(2,128)} %bitcast.6, s32[1,2]{1,0:T(1,128)} %bitcast.7, bf16[128,1024]{1,0:T(8,128)(2,1)} %q_ref.1, bf16[128,256]{1,0:T(8,128)(2,1)} %kn_ref.1, bf16[128,256]{1,0:T(8,128)(2,1)} %vn_ref.1, bf16[8,128,256]{2,1,0:T(8,128)(2,1)} %bitcast.4, bf16[8,128,256]{2,1,0:T(8,128)(2,1)} %bitcast.5, ...), custom_call_target="tpu_custom_call" | custom-call | tf_op jit(solution)/shard_map/pallas_call | solution.py:384
  61.1 1.7 %copy.10 = bf16[32,4096]{1,0:T(8,128)(2,1)} copy(bf16[32,4096]{1,0:T(8,128)(2,1)} %shard_map.82) | data formatting | bytes 524288

commit v5 on v4

--- a/solution.py
+++ b/solution.py
@@ -46,6 +46,13 @@
     base = me - mypos
     mirror = lax.rem(me + half, n)
     cols = w_v.shape[2]
+    core = lax.rem(hi, 2)
+    row = hi // 2
+    core_peer = hi + 1 - 2 * core
+    row_peer = lax.rem(hi + 2, n_head)
+    sides = (1 - row, row)
+    piece = BLOCK // n_head
+    rows_half = BLOCK // 2
 
     def w_copy(c):
         return pltpu.make_async_copy(
@@ -104,6 +111,11 @@
         remote(vn_ref, prev.at[1], prev_ss.at[1], prev_rs.at[1], {"ctx": nxt}),
     ]
 
+    for copy in prev_copies:
+        @pl.when(me < n - 1)
+        def _(copy=copy):
+            copy.start()
+
     def own_smem():
         return pltpu.make_async_copy(table.at[me], meta_s.at[me], smem_s.at[me])
 
@@ -159,11 +171,6 @@
             return 0
 
         lax.fori_loop(1, half, give, 0)
-        if x == order[0]:
-            for copy in prev_copies:
-                @pl.when(me < n - 1)
-                def _(copy=copy):
-                    copy.start()
 
     for copy_c in range(PARTS):
         w_copy(copy_c).start()
@@ -173,43 +180,47 @@
         smem_copy(mirror).wait()
         gather(mirror, recvb.at[1, mypos])
 
-    width = group * BLOCK
+    width = group * rows_half
 
     def stack(x, ref):
         for h in range(kvh):
             for j in range(group):
                 column = (h * group + j) * HD
-                qstack[x, h, j * BLOCK : (j + 1) * BLOCK, :] = ref[:, column : column + HD]
-
-    def attend(x, h, keys, values, mask):
+                for f in range(2):
+                    qstack[x, h, f, j * rows_half : (j + 1) * rows_half, :] = ref[
+                        f * rows_half : (f + 1) * rows_half, column : column + HD
+                    ]
+
+    def attend(x, h, f, keys, values, mask):
         scores = lax.dot_general(
-            keys, qstack[x, h], (((1,), (1,)), ((), ())), preferred_element_type=F32
+            keys, qstack[x, h, f], (((1,), (1,)), ((), ())), preferred_element_type=F32
         )
         scores = mask(scores)
-        old_max = stat[x, h : h + 1, :]
+        old_max = stat[x, f, h : h + 1, :]
         new_max = jnp.maximum(old_max, jnp.max(scores, axis=0, keepdims=True))
         weights = jnp.exp2((scores - new_max) * EXP2_SCALE)
         fade = jnp.exp2((old_max - new_max) * EXP2_SCALE)
-        total = stat[x, kvh + h : kvh + h + 1, :] * fade
-        stat[x, h : h + 1, :] = new_max
-        stat[x, kvh + h : kvh + h + 1, :] = total + jnp.sum(weights, axis=0, keepdims=True)
+        total = stat[x, f, kvh + h : kvh + h + 1, :] * fade
+        stat[x, f, h : h + 1, :] = new_max
+        stat[x, f, kvh + h : kvh + h + 1, :] = total + jnp.sum(weights, axis=0, keepdims=True)
         mixture = lax.dot_general(
             values, weights.astype(BF16), (((0,), (0,)), ((), ())), preferred_element_type=F32
         )
-        acc[x, h] = acc[x, h] * fade + mixture
-
-    def attend_cache(x, pi, heads=range(kvh)):
+        acc[x, h, f] = acc[x, h, f] * fade + mixture
+
+    def attend_cache(x, pi, halves=(0, 1)):
         flags = table if x == 0 else far_table
-        for h in heads:
-            two = flags[base + pi, 2 * kvh + h : 2 * kvh + h + 1, :]
-            two = jnp.concatenate([two] * group, axis=1)
-
-            def mask(scores):
-                return jnp.concatenate(
-                    [scores[:BLOCK], jnp.where(two > 0, scores[BLOCK:], NEG)], axis=0
-                )
-
-            attend(x, h, recvb[x, pi, h, 0], recvb[x, pi, h, 1], mask)
+        for f in halves:
+            for h in range(kvh):
+                two = flags[base + pi, 2 * kvh + h : 2 * kvh + h + 1, :]
+                two = jnp.concatenate([two] * (width // 128), axis=1)
+
+                def mask(scores, two=two):
+                    return jnp.concatenate(
+                        [scores[:BLOCK], jnp.where(two > 0, scores[BLOCK:], NEG)], axis=0
+                    )
+
+                attend(x, h, f, recvb[x, pi, h, 0], recvb[x, pi, h, 1], mask)
 
     def attend_arrivals(x, stop):
         def step(k, _):
@@ -220,19 +231,20 @@
 
         lax.fori_loop(1, stop, step, 0)
 
-    stat[:, 0:kvh, :] = jnp.full((GROUPS, kvh, width), NEG, F32)
-    stat[:, kvh:, :] = jnp.zeros((GROUPS, stat.shape[1] - kvh, width), F32)
+    stat[:, :, 0:kvh, :] = jnp.full((GROUPS, 2, kvh, width), NEG, F32)
+    stat[:, :, kvh:, :] = jnp.zeros((GROUPS, 2, stat.shape[2] - kvh, width), F32)
     acc[...] = jnp.zeros_like(acc)
     stack(0, q_ref)
 
-    def causal(scores):
+    def causal(f, scores):
         key = lax.broadcasted_iota(jnp.int32, scores.shape, 0)
-        row = lax.broadcasted_iota(jnp.int32, scores.shape, 1) & (BLOCK - 1)
-        return jnp.where(key <= row, scores, NEG)
+        lane = lax.broadcasted_iota(jnp.int32, scores.shape, 1)
+        return jnp.where(key <= f * rows_half + (lane & (rows_half - 1)), scores, NEG)
 
     for h in range(kvh):
         cut = slice(h * HD, (h + 1) * HD)
-        attend(0, h, kn_ref[:, cut], vn_ref[:, cut], causal)
+        for f in range(2):
+            attend(0, h, f, kn_ref[:, cut], vn_ref[:, cut], functools.partial(causal, f))
     attend_cache(0, mypos)
 
     back_copies = []
@@ -244,17 +256,23 @@
         attend_arrivals(1, half - 1)
         pi, copy = kv_recv(1, half - 1)
         copy.wait_recv()
-        for h in range(kvh):
-            attend_cache(1, pi, [h])
-            part_out[h] = acc[1, h].astype(BF16)
-            copy = remote(
-                part_out.at[h], part_in.at[h], back_ss.at[h], back_rs.at[h], {"ctx": mirror}
-            )
-            copy.start()
-            back_copies.append(copy)
-        copy = remote(stat.at[1], stat_in, back_ss.at[kvh], back_rs.at[kvh], {"ctx": mirror})
-        copy.start()
-        back_copies.append(copy)
+        for i, f in enumerate(sides):
+            attend_cache(1, pi, [f])
+            for h in range(kvh):
+                part_out[f, h] = acc[1, h, f].astype(BF16)
+            pair = [
+                remote(
+                    stat.at[1, f], stat_in.at[f], back_ss.at[i, 0], back_rs.at[i, 0],
+                    {"ctx": mirror},
+                ),
+                remote(
+                    part_out.at[f], part_in.at[f], back_ss.at[i, 1], back_rs.at[i, 1],
+                    {"ctx": mirror},
+                ),
+            ]
+            for copy in pair:
+                copy.start()
+            back_copies += pair
 
     @pl.when(me > 0)
     def _():
@@ -262,61 +280,67 @@
             copy.wait_recv()
         for h in range(kvh):
             cut = slice(h * HD, (h + 1) * HD)
-            attend(0, h, prev[0, :, cut], prev[1, :, cut], lambda scores: scores)
+            for f in range(2):
+                attend(0, h, f, prev[0, :, cut], prev[1, :, cut], lambda scores: scores)
 
     attend_arrivals(0, half)
-    for copy in back_copies:
-        copy.wait_recv()
-    for h in range(kvh):
-        own = acc[0, h]
-        total = stat[0, kvh + h : kvh + h + 1, :]
-        if GROUPS == 2:
-            here, there = stat[0, h : h + 1, :], stat_in[h : h + 1, :]
-            top = jnp.maximum(here, there)
-            fade_here = jnp.exp2((here - top) * EXP2_SCALE)
-            fade_there = jnp.exp2((there - top) * EXP2_SCALE)
-            own = own * fade_here + part_in[h].astype(F32) * fade_there
-            total = total * fade_here + stat_in[kvh + h : kvh + h + 1, :] * fade_there
-        own = own / total
-        for j in range(group):
-            column = (h * group + j) * HD
-            block = own[:, j * BLOCK : (j + 1) * BLOCK]
-            att[:, column : column + HD] = block.T.astype(BF16)
-
-    core = lax.rem(hi, 2)
-    row = hi // 2
-    core_peer = hi + 1 - 2 * core
-    row_peer = lax.rem(hi + 2, n_head)
-    piece = BLOCK // n_head
-
-    def to_core(c):
+
+    def finish(i):
+        f = sides[i]
+        for copy in back_copies[2 * i : 2 * i + 2]:
+            copy.wait_recv()
+        for h in range(kvh):
+            own = acc[0, h, f]
+            total = stat[0, f, kvh + h : kvh + h + 1, :]
+            if GROUPS == 2:
+                here, there = stat[0, f, h : h + 1, :], stat_in[f, h : h + 1, :]
+                top = jnp.maximum(here, there)
+                fade_here = jnp.exp2((here - top) * EXP2_SCALE)
+                fade_there = jnp.exp2((there - top) * EXP2_SCALE)
+                own = own * fade_here + part_in[f, h].astype(F32) * fade_there
+                total = total * fade_here + stat_in[f, kvh + h : kvh + h + 1, :] * fade_there
+            turned = (own / total).T.astype(BF16)
+            for j in range(group):
+                column = (h * group + j) * HD
+                att[i, :, column : column + HD] = turned[j * rows_half : (j + 1) * rows_half]
+
+    def to_core(c, i):
         return remote(
-            proj16.at[c, 1 - core], r1.at[c], p1_ss.at[c], p1_rs.at[c], {"head": core_peer}
+            proj16.at[c, 1 - core, i], r1.at[c, i], p1_ss.at[c, i], p1_rs.at[c, i],
+            {"head": core_peer},
         )
 
     def to_row(c):
         return remote(s2.at[c], r2.at[c], p2_ss.at[c], p2_rs.at[c], {"head": row_peer})
 
     def forward(c):
-        to_core(c).wait_recv()
-        s2[c] = (proj[c, core, 1 - row] + r1[c, 1 - row].astype(F32)).astype(BF16)
+        to_core(c, 0).wait_recv()
+        s2[c] = (proj[c, core, 0] + r1[c, 0].astype(F32)).astype(BF16)
         to_row(c).start()
 
+    def project(c, i):
+        product = jnp.dot(att[i], w_v[c], preferred_element_type=F32)
+        for side in range(2):
+            part = product[side * piece : (side + 1) * piece]
+            proj[c, side, i] = part
+            proj16[c, side, i] = part.astype(BF16)
+        to_core(c, i).start()
+
+    finish(0)
     for c in range(PARTS):
         w_copy(c).wait()
-        product = jnp.dot(att[...], w_v[c], preferred_element_type=F32)
-        for i in range(n_head):
-            rows = product[i * piece : (i + 1) * piece]
-            proj[c, i % 2, i // 2] = rows
-            proj16[c, i % 2, i // 2] = rows.astype(BF16)
-        to_core(c).start()
+        project(c, 0)
         if c > 0:
             forward(c - 1)
     forward(PARTS - 1)
+    finish(1)
     for c in range(PARTS):
+        project(c, 1)
+    for c in range(PARTS):
+        to_core(c, 1).wait_recv()
         to_row(c).wait_recv()
         out_ref[:, c * cols : (c + 1) * cols] = (
-            proj[c, core, row] + r1[c, row].astype(F32) + r2[c].astype(F32)
+            proj[c, core, 1] + r1[c, 1].astype(F32) + r2[c].astype(F32)
         ).astype(BF16)
 
     for k in range(1, n):
@@ -334,7 +358,8 @@
 
         lax.fori_loop(1, half, sent, 0)
     for c in range(PARTS):
-        to_core(c).wait_send()
+        to_core(c, 0).wait_send()
+        to_core(c, 1).wait_send()
         to_row(c).wait_send()
 
 
@@ -346,7 +371,7 @@
     kvh = keys_new.shape[1] // HD
     group = queries.shape[1] // keys_new.shape[1]
     half = n // GROUPS
-    width = group * BLOCK
+    width = group * BLOCK // 2
     d_in, d_out = out_weight.shape
     cols = d_out // PARTS
     piece = BLOCK // n_head
@@ -361,15 +386,15 @@
         pltpu.VMEM((n, 8, 128), jnp.int32),
         pltpu.VMEM(queries.shape, BF16),
         pltpu.VMEM((2,) + keys_new.shape, BF16),
-        pltpu.VMEM((GROUPS, kvh, width, HD), BF16),
+        pltpu.VMEM((GROUPS, kvh, 2, width, HD), BF16),
         pltpu.VMEM((GROUPS, half, kvh, 2, keys_slot, HD), BF16),
         pltpu.VMEM((GROUPS, half, kvh, 2, keys_slot, HD), BF16),
-        pltpu.VMEM((GROUPS, kvh, HD, width), F32),
-        pltpu.VMEM((GROUPS, 8, width), F32),
-        pltpu.VMEM((kvh, HD, width), BF16),
-        pltpu.VMEM((kvh, HD, width), BF16),
-        pltpu.VMEM((8, width), F32),
-        pltpu.VMEM((BLOCK, d_in), BF16),
+        pltpu.VMEM((GROUPS, kvh, 2, HD, width), F32),
+        pltpu.VMEM((GROUPS, 2, 8, width), F32),
+        pltpu.VMEM((2, kvh, HD, width), BF16),
+        pltpu.VMEM((2, kvh, HD, width), BF16),
+        pltpu.VMEM((2, 8, width), F32),
+        pltpu.VMEM((2, BLOCK // 2, d_in), BF16),
         pltpu.VMEM((PARTS, d_in, cols), BF16),
         pltpu.VMEM((PARTS, 2, n_head // 2, piece, cols), F32),
         pltpu.VMEM((PARTS, 2, n_head // 2, piece, cols), BF16),
@@ -378,8 +403,8 @@
         pltpu.VMEM((PARTS, piece, cols), BF16),
         dma((n,)), dma((n,)), dma((n,)),
         dma((GROUPS, half)), dma((GROUPS, half)),
-        dma((2,)), dma((2,)), dma((2,)), dma((2,)), dma((kvh + 1,)), dma((kvh + 1,)),
-        dma((PARTS,)), dma((PARTS,)), dma((PARTS,)), dma((PARTS,)), dma((PARTS,)),
+        dma((2,)), dma((2,)), dma((2,)), dma((2,)), dma((2, 2)), dma((2, 2)),
+        dma((PARTS,)), dma((PARTS, 2)), dma((PARTS, 2)), dma((PARTS,)), dma((PARTS,)),
     ]
     return pl.pallas_call(
         functools.partial(kernel, n, n_head, kvh, group),

time: 62.9 us -> 63.7 us (1.013)
  Pallas kernels: 61.1 us -> 61.9 us
    pallas_call x1, Pallas kernels: 61.1 us -> 61.9 us  [shards(): pl.pallas_call(functools.partial(kernel, n, n_head, kvh, group), out_shap...]
where the time goes in v5:
time: 63.7 us; the launch traced here: 63.6 us
  Pallas kernels  61.9 us (97%)
  local copies, waits for them, and re-layouts  1.67 us (3%)
    pallas_call x1, Pallas kernels, shards(): pl.pallas_call(functools.partial(kernel, n, n_head, kvh, group), out_shap...  61.9 us
    unnamed x1, local copies, waits for them, and re-layouts  1.67 us

profile of v5, /device:TPU:3, one launch (start us, length us, event | category | flops | bytes accessed | tf_op | source)
XLA Modules:
  0.0 63.6 jit_solution(3081551791063387263)
XLA Ops:
  0.0 61.9 %shard_map.82 = bf16[32,4096]{1,0:T(8,128)(2,1)} custom-call(s32[2,16]{1,0:T(2,128)} %bitcast.6, s32[1,2]{1,0:T(1,128)} %bitcast.7, bf16[128,1024]{1,0:T(8,128)(2,1)} %q_ref.1, bf16[128,256]{1,0:T(8,128)(2,1)} %kn_ref.1, bf16[128,256]{1,0:T(8,128)(2,1)} %vn_ref.1, bf16[8,128,256]{2,1,0:T(8,128)(2,1)} %bitcast.4, bf16[8,128,256]{2,1,0:T(8,128)(2,1)} %bitcast.5, ...), custom_call_target="tpu_custom_call" | custom-call | tf_op jit(solution)/shard_map/pallas_call | solution.py:409
  61.9 1.7 %copy.10 = bf16[32,4096]{1,0:T(8,128)(2,1)} copy(bf16[32,4096]{1,0:T(8,128)(2,1)} %shard_map.82) | data formatting | bytes 524288

commit v6 on v5

--- a/solution.py
+++ b/solution.py
@@ -111,11 +111,6 @@
         remote(vn_ref, prev.at[1], prev_ss.at[1], prev_rs.at[1], {"ctx": nxt}),
     ]
 
-    for copy in prev_copies:
-        @pl.when(me < n - 1)
-        def _(copy=copy):
-            copy.start()
-
     def own_smem():
         return pltpu.make_async_copy(table.at[me], meta_s.at[me], smem_s.at[me])
 
@@ -124,8 +119,16 @@
     def smem_copy(d):
         return pltpu.make_async_copy(meta.at[d], meta_s.at[d], smem_s.at[d])
 
+    def partner(k):
+        place, total = 1, 0
+        while place < half:
+            a, b = lax.rem(mypos // place, 2), lax.rem(k // place, 2)
+            total = total + place * (a + b - 2 * a * b)
+            place *= 2
+        return total
+
     def target(x, k):
-        pi = lax.rem(mypos + k, half)
+        pi = partner(lax.rem(half - k, half))
         p = base + pi
         d = p if x == 0 else lax.rem(p + half, n)
         return pi, p, d
@@ -145,7 +148,7 @@
         )
 
     def kv_recv(x, k):
-        pi, p, _ = target(x, half - k)
+        pi, p, _ = target(x, k)
         return pi, remote(
             sendb.at[x, pi], recvb.at[x, pi], kv_ss.at[x, pi], kv_rs.at[x, pi], {"ctx": p}
         )
@@ -171,6 +174,11 @@
             return 0
 
         lax.fori_loop(1, half, give, 0)
+        if x == order[0]:
+            for copy in prev_copies:
+                @pl.when(me < n - 1)
+                def _(copy=copy):
+                    copy.start()
 
     for copy_c in range(PARTS):
         w_copy(copy_c).start()

time: 63.7 us -> 63.8 us (level)
  no operation moved by 1% of the time
where the time goes in v6:
time: 63.8 us; the launch traced here: 63.6 us
  Pallas kernels  62 us (97%)
  local copies, waits for them, and re-layouts  1.67 us (3%)
    pallas_call x1, Pallas kernels, shards(): pl.pallas_call(functools.partial(kernel, n, n_head, kvh, group), out_shap...  62 us
    unnamed x1, local copies, waits for them, and re-layouts  1.67 us

profile of v6, /device:TPU:3, one launch (start us, length us, event | category | flops | bytes accessed | tf_op | source)
XLA Modules:
  0.0 63.6 jit_solution(8504985716924595128)
XLA Ops:
  0.0 62.0 %shard_map.82 = bf16[32,4096]{1,0:T(8,128)(2,1)} custom-call(s32[2,16]{1,0:T(2,128)} %bitcast.6, s32[1,2]{1,0:T(1,128)} %bitcast.7, bf16[128,1024]{1,0:T(8,128)(2,1)} %q_ref.1, bf16[128,256]{1,0:T(8,128)(2,1)} %kn_ref.1, bf16[128,256]{1,0:T(8,128)(2,1)} %vn_ref.1, bf16[8,128,256]{2,1,0:T(8,128)(2,1)} %bitcast.4, bf16[8,128,256]{2,1,0:T(8,128)(2,1)} %bitcast.5, ...), custom_call_target="tpu_custom_call" | custom-call | tf_op jit(solution)/shard_map/pallas_call | solution.py:417
  62.0 1.7 %copy.10 = bf16[32,4096]{1,0:T(8,128)(2,1)} copy(bf16[32,4096]{1,0:T(8,128)(2,1)} %shard_map.82) | data formatting | bytes 524288

commit v7 on v6

--- a/solution.py
+++ b/solution.py
@@ -141,16 +141,22 @@
                 dst[h, 0, s * BLOCK : (s + 1) * BLOCK, :] = ck_ref[index, :, cut]
                 dst[h, 1, s * BLOCK : (s + 1) * BLOCK, :] = cv_ref[index, :, cut]
 
+    half_of = me // half
+    top = mypos // (half // 2)
+    inner = half_of * (1 - top) + (1 - half_of) * top
+
     def kv_send(x, k):
-        pi, p, _ = target(x, k)
+        pi, p, d = target(x, k)
+        direct = x * inner * lax.div(half - k, half // 2)
         return remote(
-            sendb.at[x, pi], recvb.at[x, mypos], kv_ss.at[x, pi], kv_rs.at[x, mypos], {"ctx": p}
+            sendb.at[x, pi], recvb.at[x + direct, mypos],
+            kv_ss.at[x, pi], kv_rs.at[x + direct, mypos], {"ctx": p + direct * (d - p)},
         )
 
     def kv_recv(x, k):
-        pi, p, _ = target(x, k)
+        pi, p, _ = target(0, k)
         return pi, remote(
-            sendb.at[x, pi], recvb.at[x, pi], kv_ss.at[x, pi], kv_rs.at[x, pi], {"ctx": p}
+            sendb.at[0, pi], recvb.at[x, pi], kv_ss.at[0, pi], kv_rs.at[x, pi], {"ctx": p}
         )
 
     order = list(range(GROUPS))[::-1]
@@ -217,10 +223,11 @@
         acc[x, h, f] = acc[x, h, f] * fade + mixture
 
     def attend_cache(x, pi, halves=(0, 1)):
-        flags = table if x == 0 else far_table
+        flags = far_table if x == 1 else table
+        owner = lax.rem(base + half, n) + pi if x == 2 else base + pi
         for f in halves:
             for h in range(kvh):
-                two = flags[base + pi, 2 * kvh + h : 2 * kvh + h + 1, :]
+                two = flags[owner, 2 * kvh + h : 2 * kvh + h + 1, :]
                 two = jnp.concatenate([two] * (width // 128), axis=1)
 
                 def mask(scores, two=two):
@@ -228,16 +235,16 @@
                         [scores[:BLOCK], jnp.where(two > 0, scores[BLOCK:], NEG)], axis=0
                     )
 
-                attend(x, h, f, recvb[x, pi, h, 0], recvb[x, pi, h, 1], mask)
-
-    def attend_arrivals(x, stop):
+                attend(x % 2, h, f, recvb[x, pi, h, 0], recvb[x, pi, h, 1], mask)
+
+    def attend_arrivals(x, first, stop):
         def step(k, _):
             pi, copy = kv_recv(x, k)
             copy.wait_recv()
             attend_cache(x, pi)
             return 0
 
-        lax.fori_loop(1, stop, step, 0)
+        lax.fori_loop(first, stop, step, 0)
 
     stat[:, :, 0:kvh, :] = jnp.full((GROUPS, 2, kvh, width), NEG, F32)
     stat[:, :, kvh:, :] = jnp.zeros((GROUPS, 2, stat.shape[2] - kvh, width), F32)
@@ -261,7 +268,12 @@
             copy.wait_recv()
         stack(1, far_q)
         attend_cache(1, mypos)
-        attend_arrivals(1, half - 1)
+
+        @pl.when(inner == 1)
+        def _():
+            attend_arrivals(1, 1, half // 2 + 1)
+
+        attend_arrivals(1, half // 2 + 1, half - 1)
         pi, copy = kv_recv(1, half - 1)
         copy.wait_recv()
         for i, f in enumerate(sides):
@@ -291,7 +303,12 @@
             for f in range(2):
                 attend(0, h, f, prev[0, :, cut], prev[1, :, cut], lambda scores: scores)
 
-    attend_arrivals(0, half)
+    if GROUPS == 2:
+        @pl.when(inner == 1)
+        def _():
+            attend_arrivals(2, 1, half // 2 + 1)
+
+    attend_arrivals(0, 1, half)
 
     def finish(i):
         f = sides[i]
@@ -396,7 +413,7 @@
         pltpu.VMEM((2,) + keys_new.shape, BF16),
         pltpu.VMEM((GROUPS, kvh, 2, width, HD), BF16),
         pltpu.VMEM((GROUPS, half, kvh, 2, keys_slot, HD), BF16),
-        pltpu.VMEM((GROUPS, half, kvh, 2, keys_slot, HD), BF16),
+        pltpu.VMEM((GROUPS + 1, half, kvh, 2, keys_slot, HD), BF16),
         pltpu.VMEM((GROUPS, kvh, 2, HD, width), F32),
         pltpu.VMEM((GROUPS, 2, 8, width), F32),
         pltpu.VMEM((2, kvh, HD, width), BF16),
@@ -410,7 +427,7 @@
         pltpu.VMEM((PARTS, piece, cols), BF16),
         pltpu.VMEM((PARTS, piece, cols), BF16),
         dma((n,)), dma((n,)), dma((n,)),
-        dma((GROUPS, half)), dma((GROUPS, half)),
+        dma((GROUPS, half)), dma((GROUPS + 1, half)),
         dma((2,)), dma((2,)), dma((2,)), dma((2,)), dma((2, 2)), dma((2, 2)),
         dma((PARTS,)), dma((PARTS, 2)), dma((PARTS, 2)), dma((PARTS,)), dma((PARTS,)),
     ]

time: 63.8 us -> 61.1 us (0.958)
  the two profiles are of different devices: /device:TPU:3 before, /device:TPU:9 now
where the time goes in v7:
time: 61.1 us; the launch traced here: 60.9 us
  Pallas kernels  59.3 us (97%)
  local copies, waits for them, and re-layouts  1.67 us (3%)
    pallas_call x1, Pallas kernels, shards(): pl.pallas_call(functools.partial(kernel, n, n_head, kvh, group), out_shap...  59.3 us
    unnamed x1, local copies, waits for them, and re-layouts  1.67 us

profile of v7, /device:TPU:9, one launch (start us, length us, event | category | flops | bytes accessed | tf_op | source)
XLA Modules:
  0.0 60.9 jit_solution(7411092401991603776)
XLA Ops:
  0.0 59.3 %shard_map.82 = bf16[32,4096]{1,0:T(8,128)(2,1)} custom-call(s32[2,16]{1,0:T(2,128)} %bitcast.6, s32[1,2]{1,0:T(1,128)} %bitcast.7, bf16[128,1024]{1,0:T(8,128)(2,1)} %q_ref.1, bf16[128,256]{1,0:T(8,128)(2,1)} %kn_ref.1, bf16[128,256]{1,0:T(8,128)(2,1)} %vn_ref.1, bf16[8,128,256]{2,1,0:T(8,128)(2,1)} %bitcast.4, bf16[8,128,256]{2,1,0:T(8,128)(2,1)} %bitcast.5, ...), custom_call_target="tpu_custom_call" | custom-call | tf_op jit(solution)/shard_map/pallas_call | solution.py:434
  59.3 1.7 %copy.10 = bf16[32,4096]{1,0:T(8,128)(2,1)} copy(bf16[32,4096]{1,0:T(8,128)(2,1)} %shard_map.82) | data formatting | bytes 524288

commit v8 on v7

--- a/solution.py
+++ b/solution.py
@@ -111,6 +111,11 @@
         remote(vn_ref, prev.at[1], prev_ss.at[1], prev_rs.at[1], {"ctx": nxt}),
     ]
 
+    for copy in prev_copies:
+        @pl.when(me < n - 1)
+        def _(copy=copy):
+            copy.start()
+
     def own_smem():
         return pltpu.make_async_copy(table.at[me], meta_s.at[me], smem_s.at[me])
 
@@ -180,11 +185,6 @@
             return 0
 
         lax.fori_loop(1, half, give, 0)
-        if x == order[0]:
-            for copy in prev_copies:
-                @pl.when(me < n - 1)
-                def _(copy=copy):
-                    copy.start()
 
     for copy_c in range(PARTS):
         w_copy(copy_c).start()

time: 61.1 us -> 61.1 us (level)
  no operation moved by 1% of the time
where the time goes in v8:
time: 61.1 us; the launch traced here: 61 us
  Pallas kernels  59.3 us (97%)
  local copies, waits for them, and re-layouts  1.67 us (3%)
    pallas_call x1, Pallas kernels, shards(): pl.pallas_call(functools.partial(kernel, n, n_head, kvh, group), out_shap...  59.3 us
    unnamed x1, local copies, waits for them, and re-layouts  1.67 us

profile of v8, /device:TPU:9, one launch (start us, length us, event | category | flops | bytes accessed | tf_op | source)
XLA Modules:
  0.0 61.0 jit_solution(15079491454264427677)
XLA Ops:
  0.0 59.3 %shard_map.82 = bf16[32,4096]{1,0:T(8,128)(2,1)} custom-call(s32[2,16]{1,0:T(2,128)} %bitcast.6, s32[1,2]{1,0:T(1,128)} %bitcast.7, bf16[128,1024]{1,0:T(8,128)(2,1)} %q_ref.1, bf16[128,256]{1,0:T(8,128)(2,1)} %kn_ref.1, bf16[128,256]{1,0:T(8,128)(2,1)} %vn_ref.1, bf16[8,128,256]{2,1,0:T(8,128)(2,1)} %bitcast.4, bf16[8,128,256]{2,1,0:T(8,128)(2,1)} %bitcast.5, ...), custom_call_target="tpu_custom_call" | custom-call | tf_op jit(solution)/shard_map/pallas_call | solution.py:434
  59.3 1.7 %copy.10 = bf16[32,4096]{1,0:T(8,128)(2,1)} copy(bf16[32,4096]{1,0:T(8,128)(2,1)} %shard_map.82) | data formatting | bytes 524288

commit v9 on v8

--- a/solution.py
+++ b/solution.py
@@ -177,7 +177,8 @@
         meta_recv(mirror).wait_recv()
         smem_copy(mirror).start()
     for x in order:
-        def give(k, _, x=x):
+        def give(step, _, x=x):
+            k = half - step if x == 1 else step
             pi, _, d = target(x, k)
             smem_copy(d).wait()
             gather(d, sendb.at[x, pi])

time: 61.1 us -> 61.2 us (level)
  the two profiles are of different devices: /device:TPU:9 before, /device:TPU:19 now
where the time goes in v9:
time: 61.2 us; the launch traced here: 61 us
  Pallas kernels  59.3 us (97%)
  local copies, waits for them, and re-layouts  1.67 us (3%)
    pallas_call x1, Pallas kernels, shards(): pl.pallas_call(functools.partial(kernel, n, n_head, kvh, group), out_shap...  59.3 us
    unnamed x1, local copies, waits for them, and re-layouts  1.67 us

profile of v9, /device:TPU:19, one launch (start us, length us, event | category | flops | bytes accessed | tf_op | source)
XLA Modules:
  0.0 61.0 jit_solution(8479455385402419351)
XLA Ops:
  0.0 59.3 %shard_map.82 = bf16[32,4096]{1,0:T(8,128)(2,1)} custom-call(s32[2,16]{1,0:T(2,128)} %bitcast.6, s32[1,2]{1,0:T(1,128)} %bitcast.7, bf16[128,1024]{1,0:T(8,128)(2,1)} %q_ref.1, bf16[128,256]{1,0:T(8,128)(2,1)} %kn_ref.1, bf16[128,256]{1,0:T(8,128)(2,1)} %vn_ref.1, bf16[8,128,256]{2,1,0:T(8,128)(2,1)} %bitcast.4, bf16[8,128,256]{2,1,0:T(8,128)(2,1)} %bitcast.5, ...), custom_call_target="tpu_custom_call" | custom-call | tf_op jit(solution)/shard_map/pallas_call | solution.py:435
  59.3 1.7 %copy.10 = bf16[32,4096]{1,0:T(8,128)(2,1)} copy(bf16[32,4096]{1,0:T(8,128)(2,1)} %shard_map.82) | data formatting | bytes 524288
